TPU v7x, 256 devices: a whole 4x4x8 slice. The times are simulated.
256 devices in a mesh: outer: 8 (over z), inner: 32 (over x, y, core).
Axes of the slice: x: 4, y: 4, z: 8, core: 2. Of those that a mesh axis runs over, the one named last changes fastest.
Arguments:
- b_leaf: float32 [65536, 64], P(('outer', 'inner')), may hold values from -6 to 6
- b_sep: float32 [2048, 64], P(('outer', 'inner')), may hold values from -6 to 6
- b_root: float32 [2048, 64], P(('outer', 'inner')), may hold values from -6 to 6
- leaf_linv: float32 [65536, 256], P(('outer', 'inner')), as said below
- leaf_uinv: float32 [65536, 256], P(('outer', 'inner')), as said below
- leaf_lower: float32 [65536, 256], P(('outer', 'inner')), as said below
- leaf_upper: float32 [65536, 256], P(('outer', 'inner')), as said below
- sep_rows: int32 [256, 256], P(('outer', 'inner')), may hold values from 0 to 255, as said below
- sep_linv: float32 [2048, 256], P(('outer', 'inner')), as said below
- sep_uinv: float32 [2048, 256], P(('outer', 'inner')), as said below
- sep_lower: float32 [2048, 2048], P(None, ('outer', 'inner')), as said below
- sep_upper: float32 [2048, 2048], P(('outer', 'inner')), as said below
- root_linv: float32 [2048, 2048], P(('outer', 'inner')), as said below
- root_uinv: float32 [2048, 2048], P(('outer', 'inner')), as said below
- basis_leaf: float32 [65536, 512], P(('outer', 'inner')), as said below
- basis_sep: float32 [2048, 512], P(('outer', 'inner')), as said below
- basis_root: float32 [2048, 512], P(('outer', 'inner')), as said below
- g_blocks: float32 [262144, 128], P(('outer', 'inner')), may hold values from -0.25 to 0.25
- c_blocks: float32 [262144, 128], P(('outer', 'inner')), may hold values from -0.25 to 0.25
- block_cols: int32 [512, 4], P(('outer', 'inner')), may hold values from 0 to 1
Outputs:
- v_leaf: float32 [65536, 64], P(('outer', 'inner'))
- v_sep: float32 [2048, 64], P(('outer', 'inner'))
- v_root: float32 [2048, 64], P(('outer', 'inner'))
- coefficients: float32 [512, 64], replicated
- reduced_g: float32 [64, 64], replicated
- reduced_c: float32 [64, 64], replicated
Inputs may be any that keep to these rules, and one draw needn't show every extreme that they name: `sep_rows`: each row holds 256 distinct numbers; every row names 0 and 255. `leaf_linv`: lower triangular in each diagonal block of the stack, nonzero diagonal. `leaf_uinv`: upper triangular in each diagonal block of the stack, nonzero diagonal. `sep_linv`: lower triangular in each block of 256 rows, nonzero diagonal. `sep_uinv`: upper triangular in each block of 256 rows, nonzero diagonal. `root_linv`: lower triangular, nonzero diagonal. `root_uinv`: upper triangular, nonzero diagonal. `leaf_lower`: entries of order one over the square root of 256. `leaf_upper`: entries of order one over the square root of 256. `sep_lower`: entries of order one over the square root of the number of its columns. `sep_upper`: entries of order one over the square root of 2048. basis_leaf, basis_sep and basis_root stacked by rows form Q with Q^T Q = 69632 I up to float32 rounding. `basis_sep`: part of the stacked Q described with basis_leaf. `basis_root`: part of the stacked Q described with basis_leaf.
All inputs are finite; a program needn't handle non-finite values.
Results may differ from a plain program's by a relative error of at most 0.0003.
Values sent between devices are 32-bit elements; how exact they have to be, the bound alone decides.
A program may use at most 64 MiB of HBM per device.

v0:
```python
import jax
import jax.numpy as jnp
from jax import lax
from jax.sharding import PartitionSpec as P


def matmul_exact(left, right):
    return jnp.dot(left, right, precision=lax.Precision.HIGHEST, preferred_element_type=jnp.float32)


def contract_rows(left, right):
    return lax.dot_general(
        left,
        right,
        (((0,), (0,)), ((), ())),
        precision=lax.Precision.HIGHEST,
        preferred_element_type=jnp.float32,
    )


def shards(
    b_leaf,
    b_sep,
    b_root,
    leaf_linv,
    leaf_uinv,
    leaf_lower,
    leaf_upper,
    sep_rows,
    sep_linv,
    sep_uinv,
    sep_lower,
    sep_upper,
    root_linv,
    root_uinv,
    basis_leaf,
    basis_sep,
    basis_root,
    g_blocks,
    c_blocks,
    block_cols,
):
    ports = b_leaf.shape[1]
    sep_local = b_sep.shape[0]
    root_local = b_root.shape[0]
    sep_width = sep_linv.shape[1]
    selector = (sep_rows[0][:, None] == jnp.arange(sep_width, dtype=jnp.int32)[None, :]).astype(
        jnp.float32
    )
    y_leaf = matmul_exact(leaf_linv, b_leaf)
    contrib = matmul_exact(leaf_lower, y_leaf)
    t_sep = lax.psum_scatter(
        contract_rows(selector, contrib), "inner", scatter_dimension=0, tiled=True
    )
    sep_whole = lax.all_gather(b_sep - t_sep, "inner", axis=0, tiled=True)
    y_sep = matmul_exact(sep_linv, sep_whole)
    t_root = lax.psum_scatter(
        matmul_exact(sep_lower, y_sep), ("outer", "inner"), scatter_dimension=0, tiled=True
    )
    root_rhs = lax.all_gather(b_root - t_root, ("outer", "inner"), axis=0, tiled=True)
    y_root = matmul_exact(root_linv, root_rhs)
    y_root_all = lax.all_gather(y_root, ("outer", "inner"), axis=0, tiled=True)
    x_root = matmul_exact(root_uinv, y_root_all)
    x_root_all = lax.all_gather(x_root, ("outer", "inner"), axis=0, tiled=True)
    z_sep = y_sep - matmul_exact(sep_upper, x_root_all)
    z_sep_all = lax.all_gather(z_sep, "inner", axis=0, tiled=True)
    x_sep = matmul_exact(sep_uinv, z_sep_all)
    x_sep_all = lax.all_gather(x_sep, "inner", axis=0, tiled=True)
    coupled = matmul_exact(selector, x_sep_all)
    x_leaf = matmul_exact(leaf_uinv, y_leaf - matmul_exact(leaf_upper, coupled))
    node_count = float(
        lax.axis_size("outer") * lax.axis_size("inner") * (b_leaf.shape[0] + sep_local + root_local)
    )
    pieces_x = (x_leaf, x_sep, x_root)
    pieces_q = (basis_leaf, basis_sep, basis_root)
    projected = (
        contract_rows(basis_leaf, x_leaf)
        + contract_rows(basis_sep, x_sep)
        + contract_rows(basis_root, x_root)
    )
    coefficients = lax.psum(projected, ("outer", "inner")) / node_count
    cleaned = [
        values - matmul_exact(basis, coefficients) for basis, values in zip(pieces_q, pieces_x)
    ]
    local_gram = (
        contract_rows(cleaned[0], cleaned[0])
        + contract_rows(cleaned[1], cleaned[1])
        + contract_rows(cleaned[2], cleaned[2])
    )
    gram_matrix = lax.psum(local_gram, ("outer", "inner")) / node_count
    chol_lower = jnp.linalg.cholesky(gram_matrix)
    inverse_lower = lax.linalg.triangular_solve(
        chol_lower, jnp.eye(ports, dtype=jnp.float32), left_side=True, lower=True
    )
    v_leaf = matmul_exact(cleaned[0], inverse_lower.T)
    v_sep = matmul_exact(cleaned[1], inverse_lower.T)
    v_root = matmul_exact(cleaned[2], inverse_lower.T)
    block_rows = block_cols.shape[0]
    stored = block_cols.shape[1]
    block_size = g_blocks.shape[1]
    blocked = v_leaf.reshape(block_rows, block_size, ports)
    picked = blocked[block_cols]
    g_tiles = g_blocks.reshape(block_rows, stored, block_size, block_size)
    c_tiles = c_blocks.reshape(block_rows, stored, block_size, block_size)
    g_image = jnp.einsum("rwij,rwjp->rip", g_tiles, picked, precision=lax.Precision.HIGHEST)
    c_image = jnp.einsum("rwij,rwjp->rip", c_tiles, picked, precision=lax.Precision.HIGHEST)
    g_local = jnp.einsum("rip,riq->pq", blocked, g_image, precision=lax.Precision.HIGHEST)
    c_local = jnp.einsum("rip,riq->pq", blocked, c_image, precision=lax.Precision.HIGHEST)
    g_summed, c_summed = lax.psum((g_local, c_local), ("outer", "inner"))
    return (v_leaf, v_sep, v_root, coefficients, g_summed / node_count, c_summed / node_count)


def solution(mesh):
    return jax.shard_map(
        shards,
        mesh=mesh,
        in_specs=(
            P(("outer", "inner"), None),
            P(("outer", "inner"), None),
            P(("outer", "inner"), None),
            P(("outer", "inner"), None),
            P(("outer", "inner"), None),
            P(("outer", "inner"), None),
            P(("outer", "inner"), None),
            P(("outer", "inner"), None),
            P(("outer", "inner"), None),
            P(("outer", "inner"), None),
            P(None, ("outer", "inner")),
            P(("outer", "inner"), None),
            P(("outer", "inner"), None),
            P(("outer", "inner"), None),
            P(("outer", "inner"), None),
            P(("outer", "inner"), None),
            P(("outer", "inner"), None),
            P(("outer", "inner"), None),
            P(("outer", "inner"), None),
            P(("outer", "inner"), None),
        ),
        out_specs=(
            P(("outer", "inner"), None),
            P(("outer", "inner"), None),
            P(("outer", "inner"), None),
            P(),
            P(),
            P(),
        ),
        check_vma=False,
    )
```

profile of v0, /device:TPU:1, one launch (start us, length us, event | category | flops | bytes accessed | tf_op | source)
XLA Modules:
  0.0 1057.3 jit_solution(8577901284034292284)
XLA Ops:
  7.2 0.0 all-reduce.9.cloned.1.call-start
  7.2 1.4 fusion.16
  8.6 0.4 fusion.17
  9.0 0.7 copy-done.16
  9.7 1.0 fusion.8
  10.8 0.0 all-reduce.9.cloned.1.call-update
  10.8 0.0 all-reduce.11.cloned.1.call-start
  10.8 0.7 copy-done.20
  11.5 0.6 dynamic-slice
  12.7 112.8 %all-reduce.9.cloned.1.call-done = f32[256,64]{1,0:T(8,128)} async-done(((f32[256,64]{1,0:T(8,128)}), f32[256,64]{1,0:T(8,128)}) %all-reduce.9.cloned.1.call-update) | async-done | bytes 65552
  125.5 0.7 dynamic-slice_subtract_fusion.1
  126.2 25.7 %all_gather.18 = f32[256,64]{1,0:T(8,128)S(1)} all-gather(f32[8,64]{1,0:T(8,128)S(1)} %dynamic-slice_subtract_fusion.1), channel_id=1, replica_groups=mesh['outer'=8,'inner'=32] {'inner'}, dimensions={0}, use_global_device_ids=true | all-gather | bytes 67584 | tf_op jit(solution)/shard_map/all_gather | solution.py:55
  151.8 0.2 fusion.18
  152.0 0.7 copy-done.8
  152.7 0.6 convolution_bitcast_fusion
  153.3 1.3 copy.47
  154.7 0.0 all-reduce.7.cloned.1.call-start
  154.8 0.6 copy-done.19
  155.4 0.1 reshape.36
  155.4 251.8 %all-reduce.11.cloned.1.call-done = f32[2048,64]{1,0:T(8,128)} async-done(((f32[2048,64]{1,0:T(8,128)}), f32[2048,64]{1,0:T(8,128)}) %all-reduce.11.cloned.1.call-update) | async-done | bytes 524304
  407.2 0.7 dynamic-slice_subtract_fusion
  407.9 63.2 %all_gather.19 = f32[2048,64]{1,0:T(8,128)S(1)} all-gather(f32[8,64]{1,0:T(8,128)S(1)} %dynamic-slice_subtract_fusion), channel_id=1, replica_groups=mesh['outer'=8,'inner'=32] {'outer','inner'}, dimensions={0}, use_global_device_ids=true | all-gather | bytes 526336 | tf_op jit(solution)/shard_map/all_gather | solution.py:60
  471.1 0.7 convolution_bitcast_fusion.8
  471.7 60.2 %all_gather.20 = f32[2048,64]{1,0:T(8,128)S(1)} all-gather(f32[8,64]{1,0:T(8,128)S(1)} %convolution_bitcast_fusion.8), channel_id=1, replica_groups=mesh['outer'=8,'inner'=32] {'outer','inner'}, dimensions={0}, use_global_device_ids=true | all-gather | bytes 526336 | tf_op jit(solution)/shard_map/all_gather | solution.py:62
  532.0 0.7 fusion.19
  532.6 60.4 %all_gather.21 = f32[2048,64]{1,0:T(8,128)S(1)} all-gather(f32[8,64]{1,0:T(8,128)S(1)} %bitcast.121), channel_id=1, replica_groups=mesh['outer'=8,'inner'=32] {'outer','inner'}, dimensions={0}, use_global_device_ids=true | all-gather | bytes 526336 | tf_op jit(solution)/shard_map/all_gather | solution.py:64
  593.1 0.7 fusion.5
  593.7 23.3 %all_gather.22 = f32[256,64]{1,0:T(8,128)S(1)} all-gather(f32[8,64]{1,0:T(8,128)S(1)} %fusion.5), channel_id=1, replica_groups=mesh['outer'=8,'inner'=32] {'inner'}, dimensions={0}, use_global_device_ids=true | all-gather | bytes 67584 | tf_op jit(solution)/shard_map/all_gather | solution.py:66
  617.0 0.2 fusion.20
  617.2 23.0 %all_gather.23 = f32[256,64]{1,0:T(8,128)S(1)} all-gather(f32[8,64]{1,0:T(8,128)S(1)} %bitcast.122), channel_id=1, replica_groups=mesh['outer'=8,'inner'=32] {'inner'}, dimensions={0}, use_global_device_ids=true | all-gather | bytes 67584 | tf_op jit(solution)/shard_map/all_gather | solution.py:68
  640.2 0.3 fusion.6
  640.6 0.3 fusion.22
  640.9 0.0 copy-done.13
  640.9 0.3 fusion.23
  641.3 0.4 fusion.2
  641.6 0.4 fusion.21
  642.0 1.1 fusion.1
  643.1 237.7 %all-reduce.7.cloned.1.call-done = f32[512,64]{0,1:T(8,128)} async-done(((f32[512,64]{0,1:T(8,128)}), f32[512,64]{0,1:T(8,128)}) %all-reduce.7.cloned.1.call-update) | async-done | bytes 131088 | tf_op jit(solution)/shard_map/psum | solution.py:81
  880.8 0.9 broadcast_multiply_fusion
  881.8 0.6 convolution_subtract_fusion
  882.4 0.2 fusion.4
  882.6 0.2 fusion.3
  882.8 0.2 fusion.24
  883.0 0.2 convolution_add_fusion.2
  883.3 0.2 convolution_add_fusion.1
  883.5 76.0 %psum.29 = f32[64,64]{0,1:T(8,128)S(1)} all-reduce(f32[64,64]{0,1:T(8,128)S(1)} %convolution_add_fusion.1), channel_id=1, replica_groups=mesh['outer'=8,'inner'=32] {'outer','inner'}, use_global_device_ids=true, to_apply=%region_3.0 | all-reduce | flops 4096 | bytes 32768 | tf_op jit(solution)/shard_map/psum | solution.py:90
  959.6 0.1 copy.51
  959.7 5.8 cholesky.17
  965.6 0.6 compare_reduce_fusion
  966.2 0.7 fusion.12
  966.9 4.9 custom-call.6
  971.8 0.2 fusion.13
  972.0 0.2 fusion.25
  972.2 0.8 fusion.27
  973.0 0.8 fusion.26
  973.7 0.6 gather_fusion
  974.3 0.7 convolution_bitcast_fusion.1
  975.0 0.2 convolution_bitcast_fusion.4
  975.2 0.2 copy-done.4
  975.4 0.7 convolution_bitcast_fusion.2
  976.0 0.2 convolution_bitcast_fusion.5
  976.2 73.1 %all-reduce.2 = (f32[64,64]{0,1:T(8,128)S(1)}, f32[64,64]{0,1:T(8,128)S(1)}) all-reduce(f32[64,64]{0,1:T(8,128)S(1)} %convolution_bitcast_fusion.5, f32[64,64]{0,1:T(8,128)S(1)} %convolution_bitcast_fusion.4), channel_id=1, replica_groups=mesh['outer'=8,'inner'=32] {'outer','inner'}, use_global_device_ids=true, to_apply=%region_6.7 | all-reduce | flops 8192 | bytes 65536 | tf_op jit(solution)/shard_map/psum | solution.py:109
  1049.4 0.7 copy.57
  1050.1 0.7 copy.58
  (45 shorter events, 0.2 us)
Async XLA Ops:
  7.2 967.2 %copy-start = (f32[1024,128]{1,0:T(8,128)S(1)}, f32[1024,128]{1,0:T(8,128)}, u32[]{:S(2)}) copy-start(f32[1024,128]{1,0:T(8,128)} %param.38) | copy-start | bytes 1572868
  7.2 1.5 copy-start.6
  7.2 118.3 %all-reduce.9.cloned.1.call-start = ((), (), s32[]{:S(2)}) async-start(), calls=%async_computation.1 | async-start | bytes 262144
  9.0 0.7 copy-start.16
  10.8 396.5 %all-reduce.11.cloned.1.call-start = ((), (), s32[]{:S(2)}) async-start(), calls=%async_computation.2 | async-start | bytes 2097152
  10.8 0.7 copy-start.20
  11.5 114.0 %copy-start.17 = (f32[8,64]{1,0:T(8,128)S(1)}, f32[8,64]{1,0:T(8,128)}, u32[]{:S(2)}) copy-start(f32[8,64]{1,0:T(8,128)} %param.21) | copy-start | bytes 6148
  126.2 25.7 %copy-start.14 = (f32[8,256]{1,0:T(8,128)S(1)}, f32[8,256]{1,0:T(8,128)}, u32[]{:S(2)}) copy-start(f32[8,256]{1,0:T(8,128)} %param.28) | copy-start | bytes 24580
  151.8 0.8 copy-start.8
  154.7 0.7 copy-start.19
  154.7 252.5 %copy-start.18 = (f32[8,64]{1,0:T(8,128)S(1)}, f32[8,64]{1,0:T(8,128)}, u32[]{:S(2)}) copy-start(f32[8,64]{1,0:T(8,128)} %param.22) | copy-start | bytes 6148
  154.7 726.1 %all-reduce.7.cloned.1.call-start = ((), (), s32[]{:S(2)}) async-start(), calls=%async_computation | async-start | bytes 262144 | tf_op jit(solution)/shard_map/psum | solution.py:81
  407.9 63.2 %copy-start.9 = (f32[8,2048]{1,0:T(8,128)S(1)}, f32[8,2048]{1,0:T(8,128)}, u32[]{:S(2)}) copy-start(f32[8,2048]{1,0:T(8,128)} %param.32) | copy-start | bytes 196612
  471.7 60.2 %copy-start.10 = (f32[8,2048]{1,0:T(8,128)S(1)}, f32[8,2048]{1,0:T(8,128)}, u32[]{:S(2)}) copy-start(f32[8,2048]{1,0:T(8,128)} %param.33) | copy-start | bytes 196612
  532.6 60.4 %copy-start.11 = (f32[8,2048]{1,0:T(8,128)S(1)}, f32[8,2048]{1,0:T(8,128)}, u32[]{:S(2)}) copy-start(f32[8,2048]{1,0:T(8,128)} %param.31) | copy-start | bytes 196612
  593.7 23.3 %copy-start.15 = (f32[8,256]{1,0:T(8,128)S(1)}, f32[8,256]{1,0:T(8,128)}, u32[]{:S(2)}) copy-start(f32[8,256]{1,0:T(8,128)} %param.29) | copy-start | bytes 24580
  617.2 23.4 %copy-start.12 = (f32[8,512]{1,0:T(8,128)S(1)}, f32[8,512]{1,0:T(8,128)}, u32[]{:S(2)}) copy-start(f32[8,512]{1,0:T(8,128)} %param.35) | copy-start | bytes 49156
  640.2 0.7 copy-start.13
  640.2 1.0 copy-start.5
  640.6 1.1 copy-start.7
  640.9 1.1 copy-start.1
  881.8 0.8 copy-start.2
  972.2 3.8 copy-start.3
  974.3 1.0 copy-start.4
Sparse Core Ops, SparseCore 0:
  11.8 113.6 all-reduce.8
  154.8 252.3 all-reduce.10
  643.3 237.5 all-reduce.6
where the time goes:
time: 1060 us
  waiting for transfers between devices  602 us (57%)
  blocking collectives  405 us (38%)
  between operations  14.7 us (1%)
  other arithmetic  14.4 us (1%)
  matrix products  14 us (1%)
    unnamed x5, waiting for transfers between devices  365 us
    psum x1, waiting for transfers between devices, shards(): coefficients = lax.psum(projected, ('outer', 'inner')) / node_count  238 us
    psum x1, blocking collectives, shards(): gram_matrix = lax.psum(local_gram, ('outer', 'inner')) / node_count  76 us
    psum x1, blocking collectives, shards(): g_summed, c_summed = lax.psum((g_local, c_local), ('outer', 'inner'))  73.1 us
    all_gather x1, blocking collectives, shards(): lax.all_gather(b_root - t_root, ('outer', 'inner'), axis=0, tiled=True)  63.2 us
    all_gather x1, blocking collectives, shards(): x_root_all = lax.all_gather(x_root, ('outer', 'inner'), axis=0, tiled=True)  60.4 us
    all_gather x1, blocking collectives, shards(): y_root_all = lax.all_gather(y_root, ('outer', 'inner'), axis=0, tiled=True)  60.2 us
    all_gather x1, blocking collectives, shards(): sep_whole = lax.all_gather(b_sep - t_sep, 'inner', axis=0, tiled=True)  25.7 us
  transfers between devices with their start and end apart: 3, of which 3 were waited for; matrix products, arithmetic and copies ran while one was open for 0% of the time, Pallas kernels for 0%

commit v1 on v0

--- a/solution.py
+++ b/solution.py
@@ -87,7 +87,7 @@
         + contract_rows(cleaned[1], cleaned[1])
         + contract_rows(cleaned[2], cleaned[2])
     )
-    gram_matrix = lax.psum(local_gram, ("outer", "inner")) / node_count
+    gram_matrix = jnp.sum(lax.all_gather(local_gram, ("outer", "inner")), axis=0) / node_count
     chol_lower = jnp.linalg.cholesky(gram_matrix)
     inverse_lower = lax.linalg.triangular_solve(
         chol_lower, jnp.eye(ports, dtype=jnp.float32), left_side=True, lower=True

time: 1060 us -> 1110 us (1.047)
  waiting for transfers between devices: 602 us -> 719 us
  blocking collectives: 405 us -> 330 us
    all_gather x0 -> x1, waiting for transfers between devices: none -> 117 us  [shards(): lax.all_gather(local_gram, ('outer', 'inner'))]
    psum x1 -> x0, blocking collectives: 76 us -> none  [shards(): gram_matrix = lax.psum(local_gram, ('outer', 'inner')) / node_count]
    unnamed x5 -> x6, waiting for transfers between devices: 365 us -> 364 us
  transfers between devices with their start and end apart: 3 -> 4, of which waited for: 3 -> 4; matrix products, arithmetic and copies ran while one was open for 0% -> 0% of each run, Pallas kernels for 0% -> 0%
where the time goes in v1:
time: 1110 us
  waiting for transfers between devices  719 us (65%)
  blocking collectives  330 us (30%)
  matrix products  19.5 us (2%)
  other arithmetic  18.5 us (2%)
  between operations  14.7 us (1%)
    unnamed x6, waiting for transfers between devices  364 us
    psum x1, waiting for transfers between devices, shards(): coefficients = lax.psum(projected, ('outer', 'inner')) / node_count  237 us
    all_gather x1, waiting for transfers between devices, shards(): lax.all_gather(local_gram, ('outer', 'inner'))  117 us
    psum x1, blocking collectives, shards(): g_summed, c_summed = lax.psum((g_local, c_local), ('outer', 'inner'))  74.7 us
    all_gather x1, blocking collectives, shards(): lax.all_gather(b_root - t_root, ('outer', 'inner'), axis=0, tiled=True)  63 us
    all_gather x1, blocking collectives, shards(): x_root_all = lax.all_gather(x_root, ('outer', 'inner'), axis=0, tiled=True)  60.4 us
    all_gather x1, blocking collectives, shards(): y_root_all = lax.all_gather(y_root, ('outer', 'inner'), axis=0, tiled=True)  60.2 us
    all_gather x1, blocking collectives, shards(): sep_whole = lax.all_gather(b_sep - t_sep, 'inner', axis=0, tiled=True)  25.5 us
  transfers between devices with their start and end apart: 4, of which 4 were waited for; matrix products, arithmetic and copies ran while one was open for 0% of the time, Pallas kernels for 0%

profile of v1, /device:TPU:1, one launch (start us, length us, event | category | flops | bytes accessed | tf_op | source)
XLA Modules:
  0.0 1106.8 jit_solution(9437879770183905573)
XLA Ops:
  7.3 0.0 all-reduce.9.cloned.1.call-start
  7.3 1.5 fusion.16
  8.8 1.3 fusion.17
  10.1 1.7 fusion.8
  11.8 0.0 all-reduce.9.cloned.1.call-update
  11.9 0.0 all-reduce.11.cloned.1.call-start
  11.9 1.3 dynamic-slice
  13.8 111.8 %all-reduce.9.cloned.1.call-done = f32[256,64]{1,0:T(8,128)} async-done(((f32[256,64]{1,0:T(8,128)}), f32[256,64]{1,0:T(8,128)}) %all-reduce.9.cloned.1.call-update) | async-done | bytes 65552
  125.7 0.7 dynamic-slice_subtract_fusion.1
  126.4 25.5 %all_gather.24 = f32[256,64]{1,0:T(8,128)S(1)} all-gather(f32[8,64]{1,0:T(8,128)S(1)} %dynamic-slice_subtract_fusion.1), channel_id=1, replica_groups=mesh['outer'=8,'inner'=32] {'inner'}, dimensions={0}, use_global_device_ids=true | all-gather | bytes 67584 | tf_op jit(solution)/shard_map/all_gather | solution.py:55
  151.9 0.9 fusion.18
  152.8 1.5 convolution_bitcast_fusion
  154.2 1.4 copy.41
  155.6 0.0 all-reduce.11.cloned.1.call-update
  155.6 0.0 all-reduce.7.cloned.1.call-start
  155.7 252.5 %all-reduce.11.cloned.1.call-done = f32[2048,64]{1,0:T(8,128)} async-done(((f32[2048,64]{1,0:T(8,128)}), f32[2048,64]{1,0:T(8,128)}) %all-reduce.11.cloned.1.call-update) | async-done | bytes 524304
  408.2 0.7 dynamic-slice_subtract_fusion
  408.9 63.0 %all_gather.25 = f32[2048,64]{1,0:T(8,128)S(1)} all-gather(f32[8,64]{1,0:T(8,128)S(1)} %dynamic-slice_subtract_fusion), channel_id=1, replica_groups=mesh['outer'=8,'inner'=32] {'outer','inner'}, dimensions={0}, use_global_device_ids=true | all-gather | bytes 526336 | tf_op jit(solution)/shard_map/all_gather | solution.py:60
  471.9 1.5 convolution_bitcast_fusion.8
  473.4 60.2 %all_gather.26 = f32[2048,64]{1,0:T(8,128)S(1)} all-gather(f32[8,64]{1,0:T(8,128)S(1)} %convolution_bitcast_fusion.8), channel_id=1, replica_groups=mesh['outer'=8,'inner'=32] {'outer','inner'}, dimensions={0}, use_global_device_ids=true | all-gather | bytes 526336 | tf_op jit(solution)/shard_map/all_gather | solution.py:62
  533.7 1.5 fusion.19
  535.2 60.4 %all_gather.27 = f32[2048,64]{1,0:T(8,128)S(1)} all-gather(f32[8,64]{1,0:T(8,128)S(1)} %bitcast.123), channel_id=1, replica_groups=mesh['outer'=8,'inner'=32] {'outer','inner'}, dimensions={0}, use_global_device_ids=true | all-gather | bytes 526336 | tf_op jit(solution)/shard_map/all_gather | solution.py:64
  595.6 0.7 fusion.5
  596.2 23.2 %all_gather.28 = f32[256,64]{1,0:T(8,128)S(1)} all-gather(f32[8,64]{1,0:T(8,128)S(1)} %fusion.5), channel_id=1, replica_groups=mesh['outer'=8,'inner'=32] {'inner'}, dimensions={0}, use_global_device_ids=true | all-gather | bytes 67584 | tf_op jit(solution)/shard_map/all_gather | solution.py:66
  619.5 0.2 fusion.20
  619.6 23.0 %all_gather.29 = f32[256,64]{1,0:T(8,128)S(1)} all-gather(f32[8,64]{1,0:T(8,128)S(1)} %bitcast.124), channel_id=1, replica_groups=mesh['outer'=8,'inner'=32] {'inner'}, dimensions={0}, use_global_device_ids=true | all-gather | bytes 67584 | tf_op jit(solution)/shard_map/all_gather | solution.py:68
  642.7 0.3 fusion.6
  643.1 0.3 fusion.22
  643.4 0.3 fusion.23
  643.7 0.4 fusion.2
  644.1 0.4 fusion.21
  644.5 1.1 fusion.1
  645.6 0.0 all-reduce.7.cloned.1.call-update
  645.6 0.0 all-gather.3.cloned.1.call-start
  645.6 237.4 %all-reduce.7.cloned.1.call-done = f32[512,64]{0,1:T(8,128)} async-done(((f32[512,64]{0,1:T(8,128)}), f32[512,64]{0,1:T(8,128)}) %all-reduce.7.cloned.1.call-update) | async-done | bytes 131088 | tf_op jit(solution)/shard_map/psum | solution.py:81
  883.1 0.9 broadcast_multiply_fusion
  884.0 0.6 convolution_subtract_fusion
  884.6 0.2 fusion.4
  884.8 0.2 fusion.3
  885.0 0.2 fusion.24
  885.3 0.2 convolution_add_fusion.2
  885.5 0.9 convolution_add_fusion.1
  886.4 0.0 all-gather.3.cloned.1.call-update
  886.4 0.1 reshape.36
  886.5 117.0 %all-gather.3.cloned.1.call-done = f32[16384,64]{1,0:T(8,128)} async-done(((f32[64,64]{1,0:T(8,128)}), f32[16384,64]{1,0:T(8,128)}) %all-gather.3.cloned.1.call-update) | async-done | bytes 4194320 | tf_op jit(solution)/shard_map/all_gather | solution.py:90
  1003.6 4.0 reduce_sum.9
  1007.6 0.1 copy.42
  1007.7 0.1 copy.43
  1007.8 5.8 cholesky.17
  1013.6 0.6 compare_reduce_fusion
  1014.3 0.7 fusion.12
  1014.9 4.9 custom-call.6
  1019.8 0.2 fusion.13
  1020.1 0.2 fusion.25
  1020.3 0.8 fusion.27
  1021.1 0.8 fusion.26
  1021.8 0.6 gather_fusion
  1022.4 0.7 convolution_bitcast_fusion.1
  1023.1 0.2 convolution_bitcast_fusion.4
  1023.3 0.7 convolution_bitcast_fusion.2
  1024.0 0.2 convolution_bitcast_fusion.5
  1024.2 74.7 %all-reduce.2 = (f32[64,64]{0,1:T(8,128)S(1)}, f32[64,64]{0,1:T(8,128)S(1)}) all-reduce(f32[64,64]{0,1:T(8,128)S(1)} %convolution_bitcast_fusion.5, f32[64,64]{0,1:T(8,128)S(1)} %convolution_bitcast_fusion.4), channel_id=1, replica_groups=mesh['outer'=8,'inner'=32] {'outer','inner'}, use_global_device_ids=true, to_apply=%region_6.7 | all-reduce | flops 8192 | bytes 65536 | tf_op jit(solution)/shard_map/psum | solution.py:109
  1098.9 0.7 copy.49
  1099.6 0.7 copy.50
  (33 shorter events, 0.1 us)
Async XLA Ops:
  7.2 1015.2 %copy-start = (f32[1024,128]{1,0:T(8,128)S(1)}, f32[1024,128]{1,0:T(8,128)}, u32[]{:S(2)}) copy-start(f32[1024,128]{1,0:T(8,128)} %param.38) | copy-start | bytes 1572868
  7.2 635.5 %copy-start.11 = (s32[1,256]{1,0:T(1,128)S(1)}, s32[1,256]{1,0:T(1,128)}, u32[]{:S(2)}) copy-start(s32[1,256]{1,0:T(1,128)} %param.27) | copy-start | bytes 3076
  7.2 588.4 %copy-start.7 = (f32[8,2048]{1,0:T(8,128)S(1)}, f32[8,2048]{1,0:T(8,128)}, u32[]{:S(2)}) copy-start(f32[8,2048]{1,0:T(8,128)} %param.31) | copy-start | bytes 196612
  7.2 612.3 %copy-start.10 = (f32[8,256]{1,0:T(8,128)S(1)}, f32[8,256]{1,0:T(8,128)}, u32[]{:S(2)}) copy-start(f32[8,256]{1,0:T(8,128)} %param.29) | copy-start | bytes 24580
  7.2 635.8 %copy-start.8 = (f32[8,512]{1,0:T(8,128)S(1)}, f32[8,512]{1,0:T(8,128)}, u32[]{:S(2)}) copy-start(f32[8,512]{1,0:T(8,128)} %param.35) | copy-start | bytes 49156
  7.2 636.1 %copy-start.9 = (f32[8,512]{1,0:T(8,128)S(1)}, f32[8,512]{1,0:T(8,128)}, u32[]{:S(2)}) copy-start(f32[8,512]{1,0:T(8,128)} %param.36) | copy-start | bytes 49156
  7.2 636.5 %copy-start.5 = (f32[256,256]{1,0:T(8,128)S(1)}, f32[256,256]{1,0:T(8,128)}, u32[]{:S(2)}) copy-start(f32[256,256]{1,0:T(8,128)} %param.26) | copy-start | bytes 786436
  7.2 636.8 %copy-start.6 = (f32[256,256]{1,0:T(8,128)S(1)}, f32[256,256]{1,0:T(8,128)}, u32[]{:S(2)}) copy-start(f32[256,256]{1,0:T(8,128)} %param.24) | copy-start | bytes 786436
  7.3 637.2 %copy-start.1 = (f32[256,512]{1,0:T(8,128)S(1)}, f32[256,512]{1,0:T(8,128)}, u32[]{:S(2)}) copy-start(f32[256,512]{1,0:T(8,128)} %param.34) | copy-start | bytes 1572868
  7.3 879.1 %copy-start.12 = (s32[2,4]{1,0:T(2,128)S(1)}, s32[2,4]{1,0:T(2,128)}, u32[]{:S(2)}) copy-start(s32[2,4]{1,0:T(2,128)} %param.39) | copy-start | bytes 100
  7.3 118.4 %all-reduce.9.cloned.1.call-start = ((), (), s32[]{:S(2)}) async-start(), calls=%async_computation.2 | async-start | bytes 262144
  11.9 396.4 %all-reduce.11.cloned.1.call-start = ((), (), s32[]{:S(2)}) async-start(), calls=%async_computation.3 | async-start | bytes 2097152
  155.6 727.5 %all-reduce.7.cloned.1.call-start = ((), (), s32[]{:S(2)}) async-start(), calls=%async_computation | async-start | bytes 262144 | tf_op jit(solution)/shard_map/psum | solution.py:81
  595.6 427.7 %copy-start.4 = (f32[1024,128]{1,0:T(8,128)S(1)}, f32[1024,128]{1,0:T(8,128)}, u32[]{:S(2)}) copy-start(f32[1024,128]{1,0:T(8,128)} %param.37) | copy-start | bytes 1572868
  645.6 358.0 %all-gather.3.cloned.1.call-start = ((), (), s32[]{:S(2)}) async-start(), calls=%async_computation.1 | async-start | bytes 8421376 | tf_op jit(solution)/shard_map/all_gather | solution.py:90
  884.0 216.3 %copy-start.2 = (f32[512,64]{0,1:T(8,128)}, f32[512,64]{0,1:T(8,128)S(1)}, u32[]{:S(2)}) copy-start(f32[512,64]{0,1:T(8,128)S(1)} %broadcast_multiply_fusion) | copy-start | bytes 393220
  1020.3 80.0 %copy-start.3 = (f32[256,64]{0,1:T(8,128)}, f32[256,64]{0,1:T(8,128)S(1)}, u32[]{:S(2)}) copy-start(f32[256,64]{0,1:T(8,128)S(1)} %fusion.25) | copy-start | bytes 196612
Sparse Core Ops, SparseCore 0:
  12.0 113.6 all-reduce.8
  155.7 252.4 all-reduce.10
  645.7 237.3 all-reduce.6
  887.2 116.2 all-gather.2
